TPU v7x, 32 devices: a whole 2x2x4 slice. The times are simulated.
32 devices in a mesh: gx: 8 (over y, x, core), gy: 4 (over z).
Axes of the slice: x: 2, y: 2, z: 4, core: 2. Of those that a mesh axis runs over, the one named last changes fastest.
Arguments:
- sources: bfloat16 [8, 4, 8, 64, 256], P('gx', 'gy'), may hold values from -12 to 12
- geometry: bfloat16 [8, 4, 8, 4, 256], P('gx', 'gy'), may hold values from -0.5 to 0.5, as said below
- near_lists: int32 [8, 4, 8, 24], P('gx', 'gy'), may hold values from -1 to 255, as said below
- far_lists: int32 [8, 4, 4, 16], P('gx', 'gy'), may hold values from 0 to 7, as said below
- bases_in: bfloat16 [8, 4, 4, 32, 8, 256], P('gx', 'gy')
- bases_out: bfloat16 [8, 4, 4, 32, 8, 256], P('gx', 'gy'), may hold values from -0.25 to 0.25
- couplings: float32 [8, 4, 4, 32, 512], P('gx', 'gy')
Outputs:
- potential: float32 [8, 4, 8, 64, 256], P('gx', 'gy')
Inputs may be any that keep to these rules, and one draw needn't show every extreme that they name: `near_lists`: for each leaf the first c entries are live, c between 1 and 24 and equal to 24 on some leaves and to 1 on others; the first is the leaf itself, and every live entry names a leaf on a device whose gx and gy indices differ from the leaf's by at most one, in a slot that differs from the leaf's slot by at most one; the other entries are -1. `far_lists`: level 0 entries are below 4, levels 1 and 2 below 8, level 3 below 2. `geometry`: rows 0 to 2 lie in [-0.5, 0.5], row 3 about 0.006 to 0.04.
All inputs are finite; a program needn't handle non-finite values.
Results may differ from a plain program's by a relative error of at most 0.0029.
Values may be sent and summed in bfloat16 or wider, within the bound.
A program may use at most 64 MiB of HBM per device.

v0:
```python
import functools
import math

import jax
import jax.numpy as jnp
from jax import lax
from jax.experimental import pallas as pl
from jax.experimental.pallas import tpu as pltpu
from jax.sharding import PartitionSpec as P

FOUR_PI = 4.0 * math.pi
MESH = pl.DeviceIdType.MESH
BF16 = jnp.bfloat16
F32 = jnp.float32
FEATURES = 48


def dot(a, b, da=1, db=0):
    return lax.dot_general(a, b, (((da,), (db,)), ((), ())), preferred_element_type=F32)


def rounded(v):
    return v.astype(BF16).astype(F32)


def pieces(v):
    high = rounded(v)
    mid = rounded(v - high)
    return high, mid, rounded(v - high - mid)


def total(terms):
    return functools.reduce(jnp.add, terms)


def kernel(
    n_gx, n_gy, src_in, geo, near, far, in_in, out_in, coup_in, out,
    hsrc, gbuf, gf, lists, weight, sfeat, tfeat, acc, res, rbuf,
    base_in, base_out, flat, by_leaf, coup,
    proj, col_buf, row_src, row_buf, tab3, gath, int_src, int_buf, c3_src, c3_buf, target,
    load, geo_s, geo_r, list_s, list_r, src_s, src_r, res_s, res_r,
    p1_s, p1_r, p2_s, p2_r, p3_s, p3_r, p4_s, p4_r,
):
    x = lax.axis_index("gx")
    y = lax.axis_index("gy")
    leaf_dev, rhs, panels = out.shape
    slots = near.shape[1]
    barrier = pltpu.get_barrier_semaphore()
    for k in range(1, n_gx):
        pl.semaphore_signal(
            barrier, inc=1, device_id=(lax.rem(x + k, n_gx), y), device_id_type=MESH
        )
    for k in range(1, n_gy):
        pl.semaphore_signal(
            barrier, inc=1, device_id=(x, lax.rem(y + k, n_gy)), device_id_type=MESH
        )

    loads = [
        pltpu.make_async_copy(a, b, load.at[i])
        for i, (a, b) in enumerate(
            [(src_in, hsrc.at[1]), (in_in, base_in), (coup_in, coup), (out_in, base_out)]
        )
    ]
    for one in loads:
        one.start()

    def remote(src, dst, send, recv, where):
        return pltpu.make_async_remote_copy(
            src_ref=src, dst_ref=dst, send_sem=send, recv_sem=recv,
            device_id=where, device_id_type=MESH,
        )

    def has(d, at, n):
        return at > 0 if d < 0 else at < n - 1

    sides = (-1, 1)

    def geo_y(d):
        return remote(gbuf.at[1], gbuf.at[1 - d], geo_s.at[1 + d], geo_r.at[1 - d], (x, y + d))

    def geo_x(d):
        return remote(
            gbuf.at[1], gbuf.at[4 - d], geo_s.at[4 + d], geo_r.at[4 - d], (x + d, y)
        )

    def list_x(d):
        return remote(lists.at[1], lists.at[1 - d], list_s.at[1 + d], list_r.at[1 - d], (x + d, y))

    def src_y(d):
        return remote(hsrc.at[1], hsrc.at[1 - d], src_s.at[1 + d], src_r.at[1 - d], (x, y + d))

    def res_x(d):
        return remote(res.at[1 + d], rbuf.at[1 - d], res_s.at[1 + d], res_r.at[1 - d], (x + d, y))

    def arrived(make, d):
        if make is geo_y:
            c = remote(gbuf.at[1], gbuf.at[1 + d], geo_s.at[1 + d], geo_r.at[1 + d], (x, y + d))
        elif make is geo_x:
            c = remote(gbuf.at[1], gbuf.at[4 + d], geo_s.at[4 + d], geo_r.at[4 + d], (x + d, y))
        elif make is list_x:
            c = remote(
                lists.at[1], lists.at[1 + d], list_s.at[1 + d], list_r.at[1 + d], (x + d, y)
            )
        elif make is src_y:
            c = remote(hsrc.at[1], hsrc.at[1 + d], src_s.at[1 + d], src_r.at[1 + d], (x, y + d))
        else:
            c = remote(res.at[1 + d], rbuf.at[1 + d], res_s.at[1 + d], res_r.at[1 + d], (x + d, y))
        c.wait_recv()

    def column(src, buf, send, recv):
        for k in range(1, n_gy):
            to = lax.rem(y + k, n_gy)
            remote(src, buf.at[y], send.at[k], recv.at[y], (x, to)).start()
        buf[y] = src[...]

    def column_wait(src, buf, send, recv):
        for k in range(1, n_gy):
            peer = lax.rem(y + k, n_gy)
            remote(src, buf.at[peer], send.at[k], recv.at[peer], (x, peer)).wait_recv()

    row_at = lax.broadcasted_iota(jnp.int32, (8, panels), 0)
    quarter = 4 * (y // 4)
    half = rhs
    base = 4 * (x // 4)
    spot = lax.rem(x, 4)

    own = geo[...].astype(F32)
    own = jnp.concatenate([own, jnp.zeros((leaf_dev, 4, panels), F32)], axis=1)
    own = own.reshape(8 * leaf_dev, panels)
    gbuf[1] = own.astype(BF16)
    gf[1] = own
    lists[1] = jnp.full(lists.shape[1:], -1, jnp.int32)
    lists[1, :, 0:slots] = near[...]

    def source_features(place):
        shift = lax.convert_element_type(place - 1, F32)

        def leaf(k, carry):
            q = gf[place, pl.ds(pl.multiple_of(8 * k, 8), 8), :]
            q = jnp.where(row_at == 1, q + shift, q)
            area = q[3:4]
            factor = FOUR_PI / area
            factor = factor * factor
            square = q[0:1] * q[0:1] + q[1:2] * q[1:2] + q[2:3] * q[2:3] + area
            one = jnp.where(row_at == 4, 1.0, 0.0)
            v = jnp.where(row_at < 3, q, jnp.where(row_at == 3, square, one)) * factor
            a, b, c = pieces(v)
            wide = jnp.concatenate([a, b, c, a, b, a], axis=0)
            sfeat[place * leaf_dev + k] = wide.T.astype(BF16)
            return carry

        lax.fori_loop(0, leaf_dev, leaf, 0)

    def target_features(side, at):
        def leaf(l, carry):
            p = gf[at, pl.ds(pl.multiple_of(8 * l, 8), 8), :]
            p = jnp.where(row_at == 0, p + float(side), p)
            for dz in (-1, 0, 1):
                t = jnp.where(row_at == 2, p - float(dz), p)
                square = t[0:1] * t[0:1] + t[1:2] * t[1:2] + t[2:3] * t[2:3]
                last = jnp.where(row_at == 4, square, 0.0)
                v = jnp.where(row_at < 3, -2.0 * t, jnp.where(row_at == 3, 1.0, last))
                a, b, c = pieces(v)
                wide = jnp.concatenate([a, a, a, b, b, c], axis=0)
                tfeat[((side + 1) * leaf_dev + l) * 3 + dz + 1] = wide.astype(BF16)
            return carry

        lax.fori_loop(0, leaf_dev, leaf, 0)

    def weights(side):
        mine = lists[side + 1]
        leaf = lax.broadcasted_iota(jnp.int32, mine.shape, 0)
        for s in range(3):
            for dz in (-1, 0, 1):
                n = (x * n_gy + y + s - 1) * leaf_dev + dz + leaf
                hits = jnp.where(mine == n, 1.0, 0.0)
                count = jnp.sum(hits, axis=1, keepdims=True)
                weight[((side + 1) * 3 + s) * 3 + dz + 1] = jnp.broadcast_to(
                    count, (leaf_dev, panels)
                )

    def transposed(source, take):
        wide = source[...].astype(F32)
        for h in range(panels // 128):
            flat[h] = wide[:, 128 * h : 128 * (h + 1)]
        for k in range(leaf_dev):
            take(
                k,
                jnp.concatenate(
                    [
                        flat[h, pl.ds(k, 128, stride=leaf_dev), :]
                        for h in range(panels // 128)
                    ],
                    axis=1,
                ).astype(BF16),
            )

    loads[0].wait()
    loads[1].wait()
    parts = []
    transposed(base_in, lambda k, b: parts.append(dot(b, hsrc[1, k], 1, 1)))
    projection = total(parts)
    proj[:, 0:half] = projection[0:64]
    proj[:, half:] = projection[64:128]

    pl.semaphore_wait(barrier, n_gx - 1 + n_gy - 1)
    column(proj, col_buf, p1_s, p1_r)
    for d in sides:
        @pl.when(has(d, x, n_gx))
        def _():
            geo_x(d).start()
            list_x(d).start()

        @pl.when(has(d, y, n_gy))
        def _():
            geo_y(d).start()
            src_y(d).start()

    source_features(1)
    target_features(0, 1)
    weights(0)
    acc[...] = jnp.zeros_like(acc)
    for d in sides:
        @pl.when(jnp.logical_not(has(d, x, n_gx)))
        def _():
            rbuf[1 + d] = jnp.zeros(rbuf.shape[1:], BF16)

    def coupled(level):
        c = coup[level]
        c_high = c.astype(BF16)
        c_low = (c - c_high.astype(F32)).astype(BF16)
        g = gath[...]
        g_high = g.astype(BF16)
        g_low = (g - g_high.astype(F32)).astype(BF16)
        return dot(c_high, g_high) + (dot(c_low, g_high) + dot(c_high, g_low))

    def after_first():
        column_wait(proj, col_buf, p1_s, p1_r)
        row_src[0:32, 0:half] = total([col_buf[quarter + g, 32:64, 0:half] for g in range(4)])
        coarse = total([col_buf[g, :, half:] for g in range(n_gy)])
        row_src[0:32, half:] = coarse[0:32]
        row_src[32:48, 0:half] = coarse[32:48]
        row_src[32:48, half:] = coarse[48:64]
        for k in range(1, n_gx):
            to = lax.rem(x + k, n_gx)
            remote(row_src, row_buf.at[x], p2_s.at[k], p2_r.at[x], (to, y)).start()
        row_buf[x] = row_src[...]
        loads[2].wait()
        for m in range(16):
            gath[pl.ds(m * 32, 32), :] = col_buf[far[0, m], 0:32, 0:half]
        target[0:32, :] = coupled(0)

    def after_second():
        for k in range(1, n_gx):
            peer = lax.rem(x + k, n_gx)
            remote(row_src, row_buf.at[peer], p2_s.at[k], p2_r.at[peer], (peer, y)).wait_recv()
        for c in range(n_gx // 4):
            coarse = total([row_buf[4 * c + g, 32:48, :] for g in range(4)])
            tab3[c, 0:16, :] = coarse[:, 0:half]
            tab3[c, 16:32, :] = coarse[:, half:]
        for level in (1, 2, 3):
            for m in range(16):
                s = far[level, m]
                if level == 3:
                    gath[pl.ds(m * 32, 32), :] = tab3[s]
                elif level == 1:
                    gath[pl.ds(m * 32, 32), :] = row_buf[s, 0:32, 0:half]
                else:
                    gath[pl.ds(m * 32, 32), :] = row_buf[s, 0:32, half:]
            term = coupled(level)
            if level == 1:
                int_src[0:32, 0:half] = term
            elif level == 2:
                int_src[0:32, half:] = term
            else:
                int_src[32:48, 0:half] = term[0:16]
                int_src[32:48, half:] = term[16:32]
        column(int_src, int_buf, p3_s, p3_r)

    def after_third():
        column_wait(int_src, int_buf, p3_s, p3_r)
        c3_src[...] = total([int_buf[g, 32:48, :] for g in range(n_gy)])
        for k in range(1, 4):
            to = base + lax.rem(spot + k, 4)
            remote(c3_src, c3_buf.at[spot], p4_s.at[k], p4_r.at[spot], (to, y)).start()
        c3_buf[spot] = c3_src[...]
        target[32:64, :] = total([int_buf[quarter + g, 0:32, 0:half] for g in range(4)])
        target[64:96, :] = total([int_buf[g, 0:32, half:] for g in range(n_gy)])

    def after_fourth():
        for k in range(1, 4):
            peer = lax.rem(spot + k, 4)
            remote(
                c3_src, c3_buf.at[peer], p4_s.at[k], p4_r.at[peer], (base + peer, y)
            ).wait_recv()
        coarse = total([c3_buf[g] for g in range(4)])
        target[96:112, :] = coarse[:, 0:half]
        target[112:128, :] = coarse[:, half:]
        loads[3].wait()

        def take(k, b):
            by_leaf[k] = b

        transposed(base_out, take)

    def from_row():
        for d in sides:
            @pl.when(has(d, x, n_gx))
            def _():
                arrived(geo_x, d)
                arrived(list_x, d)
                gf[4 + d] = gbuf[4 + d].astype(F32)
                target_features(d, 4 + d)
                weights(d)

    def from_column():
        for d in sides:
            @pl.when(has(d, y, n_gy))
            def _():
                arrived(geo_y, d)
                gf[1 + d] = gbuf[1 + d].astype(F32)
                source_features(1 + d)
                arrived(src_y, d)

    def give(d):
        @pl.when(has(d, x, n_gx))
        def _():
            res[1 + d] = acc[1 + d].astype(BF16)
            res_x(d).start()

    def chunk(s, t):
        for l in range(leaf_dev):
            ks = [k for k in (l - 1, l, l + 1) if 0 <= k < leaf_dev]
            mats = []
            for k in ks:
                dz = k - l
                squared = dot(sfeat[s * leaf_dev + k], tfeat[(t * leaf_dev + l) * 3 + dz + 1])
                w = weight[(t * 3 + s) * 3 + dz + 1, l : l + 1, :]
                mats.append((lax.rsqrt(squared) * w).astype(BF16))
            wide = jnp.concatenate([hsrc[s, k] for k in ks], axis=1)
            acc[t, l] += dot(wide, jnp.concatenate(mats, axis=0))

    def step(c, carry):
        stages = {
            1: [from_row],
            2: [after_first],
            3: [from_column, after_second],
            5: [lambda: give(1), after_third],
            7: [lambda: give(-1), after_fourth],
        }
        for at, work in stages.items():
            @pl.when(c == at)
            def _():
                for one in work:
                    one()

        s = jnp.where(c < 3, 1, 2 * lax.rem(c, 2))
        late = jnp.where(c < 5, 2, jnp.where(c < 7, 0, 1))
        t = jnp.where(c == 0, 1, jnp.where(c == 2, 0, late))
        at_x, at_y = x + t - 1, y + s - 1
        inside = jnp.logical_and(
            jnp.logical_and(at_x >= 0, at_x < n_gx), jnp.logical_and(at_y >= 0, at_y < n_gy)
        )

        @pl.when(inside)
        def _():
            chunk(s, t)

        return carry

    lax.fori_loop(0, 9, step, 0)

    turned = target[...].T.astype(BF16)
    for d in sides:
        @pl.when(has(d, x, n_gx))
        def _():
            arrived(res_x, d)
    for k in range(leaf_dev):
        near_field = acc[1, k] + (rbuf[0, k].astype(F32) + rbuf[2, k].astype(F32))
        out[k] = near_field + dot(turned, by_leaf[k])

    for d in sides:
        @pl.when(has(d, x, n_gx))
        def _():
            geo_x(d).wait_send()
            list_x(d).wait_send()
            res_x(d).wait_send()

        @pl.when(has(d, y, n_gy))
        def _():
            geo_y(d).wait_send()
            src_y(d).wait_send()
    for k in range(1, n_gy):
        to = lax.rem(y + k, n_gy)
        remote(proj, col_buf.at[y], p1_s.at[k], p1_r.at[y], (x, to)).wait_send()
        remote(int_src, int_buf.at[y], p3_s.at[k], p3_r.at[y], (x, to)).wait_send()
    for k in range(1, n_gx):
        to = lax.rem(x + k, n_gx)
        remote(row_src, row_buf.at[x], p2_s.at[k], p2_r.at[x], (to, y)).wait_send()
    for k in range(1, 4):
        to = base + lax.rem(spot + k, 4)
        remote(c3_src, c3_buf.at[spot], p4_s.at[k], p4_r.at[spot], (to, y)).wait_send()


def body(sources, geometry, near_lists, far_lists, bases_in, bases_out, couplings):
    leaf_dev, rhs, panels = sources.shape[2:]
    n_gx, n_gy = lax.axis_size("gx"), lax.axis_size("gy")
    vmem = pl.BlockSpec(memory_space=pltpu.VMEM)
    anywhere = pl.BlockSpec(memory_space=pl.ANY)
    sems = pltpu.SemaphoreType.DMA
    flat_rows = bases_in.shape[2] * bases_in.shape[3] * leaf_dev
    potential = pl.pallas_call(
        functools.partial(kernel, n_gx, n_gy),
        out_shape=jax.ShapeDtypeStruct((leaf_dev, rhs, panels), F32),
        in_specs=[
            anywhere, vmem, vmem, pl.BlockSpec(memory_space=pltpu.SMEM),
            anywhere, anywhere, anywhere,
        ],
        out_specs=vmem,
        scratch_shapes=[
            pltpu.VMEM((3, leaf_dev, rhs, panels), BF16),
            pltpu.VMEM((6, 8 * leaf_dev, panels), BF16),
            pltpu.VMEM((6, 8 * leaf_dev, panels), F32),
            pltpu.VMEM((3, leaf_dev, 128), jnp.int32),
            pltpu.VMEM((27, leaf_dev, panels), F32),
            pltpu.VMEM((3 * leaf_dev, panels, FEATURES), BF16),
            pltpu.VMEM((9 * leaf_dev, FEATURES, panels), BF16),
            pltpu.VMEM((3, leaf_dev, rhs, panels), F32),
            pltpu.VMEM((3, leaf_dev, rhs, panels), BF16),
            pltpu.VMEM((3, leaf_dev, rhs, panels), BF16),
            pltpu.VMEM((flat_rows, panels), BF16),
            pltpu.VMEM((flat_rows, panels), BF16),
            pltpu.VMEM((panels // 128, flat_rows, 128), F32),
            pltpu.VMEM((leaf_dev, 128, panels), BF16),
            pltpu.VMEM(couplings.shape[2:], F32),
            pltpu.VMEM((64, 2 * rhs), F32),
            pltpu.VMEM((n_gy, 64, 2 * rhs), F32),
            pltpu.VMEM((48, 2 * rhs), F32),
            pltpu.VMEM((n_gx, 48, 2 * rhs), F32),
            pltpu.VMEM((n_gx // 4, 32, rhs), F32),
            pltpu.VMEM((512, rhs), F32),
            pltpu.VMEM((48, 2 * rhs), F32),
            pltpu.VMEM((n_gy, 48, 2 * rhs), F32),
            pltpu.VMEM((16, 2 * rhs), F32),
            pltpu.VMEM((4, 16, 2 * rhs), F32),
            pltpu.VMEM((128, rhs), F32),
            sems((4,)),
            sems((6,)), sems((6,)), sems((3,)), sems((3,)),
            sems((3,)), sems((3,)), sems((3,)), sems((3,)),
            sems((n_gy,)), sems((n_gy,)),
            sems((n_gx,)), sems((n_gx,)),
            sems((n_gy,)), sems((n_gy,)),
            sems((4,)), sems((4,)),
        ],
        compiler_params=pltpu.CompilerParams(
            collective_id=0, has_side_effects=True, vmem_limit_bytes=40 * 1024 * 1024
        ),
    )(
        sources[0, 0], geometry[0, 0], near_lists[0, 0], far_lists[0, 0],
        bases_in.reshape(flat_rows, panels), bases_out.reshape(flat_rows, panels),
        couplings[0, 0],
    )
    return potential.reshape(sources.shape)


def solution(mesh):
    in_specs = (
        P("gx", "gy", None, None, None),
        P("gx", "gy", None, None, None),
        P("gx", "gy", None, None),
        P("gx", "gy", None, None),
        P("gx", "gy", None, None, None, None),
        P("gx", "gy", None, None, None, None),
        P("gx", "gy", None, None, None),
    )
    out_specs = P("gx", "gy", None, None, None)
    return jax.shard_map(body, mesh=mesh, in_specs=in_specs, out_specs=out_specs, check_vma=False)
```

profile of v0, /device:TPU:11, one launch (start us, length us, event | category | flops | bytes accessed | tf_op | source)
XLA Modules:
  0.0 35.9 jit_solution(5454810029936506159)
XLA Ops:
  0.0 0.0 copy-start.5
  0.0 0.0 copy-start.6
  0.0 0.7 %copy-done.5 = s32[1,1,8,24]{3,2,1,0:T(8,128)S(1)} copy-done((s32[1,1,8,24]{3,2,1,0:T(8,128)S(1)}, s32[1,1,8,24]{3,2,1,0:T(8,128)}, u32[]{:S(2)}) %copy-start.5) | copy-done | bytes 792
  0.7 0.0 copy-done.6
  0.7 0.0 copy-start
  0.7 1.0 %copy-done = bf16[1,1,4,32,8,256]{5,4,3,2,1,0:T(8,128)(2,1)S(1)} copy-done((bf16[1,1,4,32,8,256]{5,4,3,2,1,0:T(8,128)(2,1)S(1)}, bf16[1,1,4,32,8,256]{5,4,3,2,1,0:T(8,128)(2,1)}, u32[]{:S(2)}) %copy-start) | copy-done | bytes 524312
  1.7 0.0 copy-start.1
  1.7 1.0 %copy-done.1 = bf16[1,1,4,32,8,256]{5,4,3,2,1,0:T(8,128)(2,1)S(1)} copy-done((bf16[1,1,4,32,8,256]{5,4,3,2,1,0:T(8,128)(2,1)S(1)}, bf16[1,1,4,32,8,256]{5,4,3,2,1,0:T(8,128)(2,1)}, u32[]{:S(2)}) %copy-start.1) | copy-done | bytes 524312
  2.8 0.0 copy-start.2
  2.8 0.9 %copy-done.2 = bf16[1,1,8,64,256]{4,3,2,1,0:T(8,128)(2,1)S(1)} copy-done((bf16[1,1,8,64,256]{4,3,2,1,0:T(8,128)(2,1)S(1)}, bf16[1,1,8,64,256]{4,3,2,1,0:T(8,128)(2,1)}, u32[]{:S(2)}) %copy-start.2) | copy-done | bytes 262168
  3.7 0.0 copy-start.3
  3.7 0.9 %copy-done.3 = f32[1,1,4,32,512]{4,3,2,1,0:T(8,128)S(1)} copy-done((f32[1,1,4,32,512]{4,3,2,1,0:T(8,128)S(1)}, f32[1,1,4,32,512]{4,3,2,1,0:T(8,128)}, u32[]{:S(2)}) %copy-start.3) | copy-done | bytes 262168
  4.7 0.0 copy-start.4
  4.7 0.7 %copy-done.4 = bf16[1,1,8,4,256]{4,3,2,1,0:T(4,128)(2,1)S(1)} copy-done((bf16[1,1,8,4,256]{4,3,2,1,0:T(4,128)(2,1)S(1)}, bf16[1,1,8,4,256]{4,3,2,1,0:T(4,128)(2,1)}, u32[]{:S(2)}) %copy-start.4) | copy-done | bytes 16408
  5.4 29.7 %shard_map.73 = f32[8,64,256]{2,1,0:T(8,128)S(1)} custom-call(bf16[8,64,256]{2,1,0:T(8,128)(2,1)S(1)} %bitcast.11, bf16[8,4,256]{2,1,0:T(4,128)(2,1)S(1)} %bitcast.13, s32[8,24]{1,0:T(8,128)S(1)} %bitcast.14, s32[4,16]{1,0:T(4,128)S(1)} %bitcast.15, bf16[1024,256]{1,0:T(8,128)(2,1)S(1)} %bitcast.9, bf16[1024,256]{1,0:T(8,128)(2,1)S(1)} %bitcast.10, ...), custom_call_target="tpu_custom_call" | custom-call | tf_op jit(solution)/shard_map/pallas_call | solution.py:412
  35.1 0.8 %copy.9 = f32[1,1,8,64,256]{4,3,2,1,0:T(8,128)} copy(f32[1,1,8,64,256]{4,3,2,1,0:T(8,128)S(1)} %bitcast.8) | data formatting | bytes 1048576
Async XLA Ops:
  0.0 0.7 %copy-start.5 = (s32[1,1,8,24]{3,2,1,0:T(8,128)S(1)}, s32[1,1,8,24]{3,2,1,0:T(8,128)}, u32[]{:S(2)}) copy-start(s32[1,1,8,24]{3,2,1,0:T(8,128)} %param.9) | copy-start | bytes 2308
  0.0 0.7 %copy-start.6 = (s32[1,1,4,16]{3,2,1,0:T(4,128)S(1)}, s32[1,1,4,16]{3,2,1,0:T(4,128)}, u32[]{:S(2)}) copy-start(s32[1,1,4,16]{3,2,1,0:T(4,128)} %param.10) | copy-start | bytes 772
  0.7 1.0 %copy-start = (bf16[1,1,4,32,8,256]{5,4,3,2,1,0:T(8,128)(2,1)S(1)}, bf16[1,1,4,32,8,256]{5,4,3,2,1,0:T(8,128)(2,1)}, u32[]{:S(2)}) copy-start(bf16[1,1,4,32,8,256]{5,4,3,2,1,0:T(8,128)(2,1)} %param.11) | copy-start | bytes 1572868
  1.7 1.0 %copy-start.1 = (bf16[1,1,4,32,8,256]{5,4,3,2,1,0:T(8,128)(2,1)S(1)}, bf16[1,1,4,32,8,256]{5,4,3,2,1,0:T(8,128)(2,1)}, u32[]{:S(2)}) copy-start(bf16[1,1,4,32,8,256]{5,4,3,2,1,0:T(8,128)(2,1)} %param.12) | copy-start | bytes 1572868
  2.8 0.9 %copy-start.2 = (bf16[1,1,8,64,256]{4,3,2,1,0:T(8,128)(2,1)S(1)}, bf16[1,1,8,64,256]{4,3,2,1,0:T(8,128)(2,1)}, u32[]{:S(2)}) copy-start(bf16[1,1,8,64,256]{4,3,2,1,0:T(8,128)(2,1)} %param.7) | copy-start | bytes 786436
  3.7 0.9 %copy-start.3 = (f32[1,1,4,32,512]{4,3,2,1,0:T(8,128)S(1)}, f32[1,1,4,32,512]{4,3,2,1,0:T(8,128)}, u32[]{:S(2)}) copy-start(f32[1,1,4,32,512]{4,3,2,1,0:T(8,128)} %param.13) | copy-start | bytes 786436
  4.7 0.7 %copy-start.4 = (bf16[1,1,8,4,256]{4,3,2,1,0:T(4,128)(2,1)S(1)}, bf16[1,1,8,4,256]{4,3,2,1,0:T(4,128)(2,1)}, u32[]{:S(2)}) copy-start(bf16[1,1,8,4,256]{4,3,2,1,0:T(4,128)(2,1)} %param.8) | copy-start | bytes 49156
where the time goes:
time: 36.2 us; the launch traced here: 35.9 us
  Pallas kernels  29.7 us (82%)
  local copies, waits for them, and re-layouts  6.19 us (17%)
    pallas_call x1, Pallas kernels, body(): pl.pallas_call(functools.partial(kernel, n_gx, n_gy), out_shape=jax.Shape...  29.7 us
    unnamed x15, local copies, waits for them, and re-layouts  6.19 us

commit v1 on v0

--- a/solution.py
+++ b/solution.py
@@ -34,10 +34,10 @@
 
 
 def kernel(
-    n_gx, n_gy, src_in, geo, near, far, in_in, out_in, coup_in, out,
-    hsrc, gbuf, gf, lists, weight, sfeat, tfeat, acc, res, rbuf,
+    n_gx, n_gy, src_in, geo_in, near_in, far, in_in, out_in, coup_in, out,
+    geo, near, hsrc, gbuf, gf, lists, weight, sfeat, tfeat, acc, res, rbuf,
     base_in, base_out, flat, by_leaf, coup,
-    proj, col_buf, row_src, row_buf, tab3, gath, int_src, int_buf, c3_src, c3_buf, target,
+    mats, proj, col_buf, row_src, row_buf, tab3, gath, int_src, int_buf, c3_src, c3_buf, target,
     load, geo_s, geo_r, list_s, list_r, src_s, src_r, res_s, res_r,
     p1_s, p1_r, p2_s, p2_r, p3_s, p3_r, p4_s, p4_r,
 ):
@@ -45,6 +45,8 @@
     y = lax.axis_index("gy")
     leaf_dev, rhs, panels = out.shape
     slots = near.shape[1]
+    middle = leaf_dev // 2
+    first = middle + 1
     barrier = pltpu.get_barrier_semaphore()
     for k in range(1, n_gx):
         pl.semaphore_signal(
@@ -58,7 +60,7 @@
     loads = [
         pltpu.make_async_copy(a, b, load.at[i])
         for i, (a, b) in enumerate(
-            [(src_in, hsrc.at[1]), (in_in, base_in), (coup_in, coup), (out_in, base_out)]
+            [(src_in, hsrc.at[1]), (in_in, base_in), (coup_in, coup), (out_in, base_out), (geo_in, geo), (near_in, near)]
         )
     ]
     for one in loads:
@@ -86,13 +88,21 @@
     def list_x(d):
         return remote(lists.at[1], lists.at[1 - d], list_s.at[1 + d], list_r.at[1 - d], (x + d, y))
 
-    def src_y(d):
-        return remote(hsrc.at[1], hsrc.at[1 - d], src_s.at[1 + d], src_r.at[1 - d], (x, y + d))
-
-    def res_x(d):
-        return remote(res.at[1 + d], rbuf.at[1 - d], res_s.at[1 + d], res_r.at[1 - d], (x + d, y))
-
-    def arrived(make, d):
+    def src_y(d, h):
+        part = pl.ds(first * h, first if h == 0 else leaf_dev - first)
+        return remote(
+            hsrc.at[1, part], hsrc.at[1 - d, part],
+            src_s.at[1 + d, h], src_r.at[1 - d, h], (x, y + d),
+        )
+
+    def res_x(d, h):
+        part = pl.ds(middle * h, middle)
+        return remote(
+            res.at[1 + d, part], rbuf.at[1 - d, part],
+            res_s.at[1 + d, h], res_r.at[1 - d, h], (x + d, y),
+        )
+
+    def arrived(make, d, h=0):
         if make is geo_y:
             c = remote(gbuf.at[1], gbuf.at[1 + d], geo_s.at[1 + d], geo_r.at[1 + d], (x, y + d))
         elif make is geo_x:
@@ -102,9 +112,17 @@
                 lists.at[1], lists.at[1 + d], list_s.at[1 + d], list_r.at[1 + d], (x + d, y)
             )
         elif make is src_y:
-            c = remote(hsrc.at[1], hsrc.at[1 + d], src_s.at[1 + d], src_r.at[1 + d], (x, y + d))
+            part = pl.ds(first * h, first if h == 0 else leaf_dev - first)
+            c = remote(
+                hsrc.at[1, part], hsrc.at[1 + d, part],
+                src_s.at[1 + d, h], src_r.at[1 + d, h], (x, y + d),
+            )
         else:
-            c = remote(res.at[1 + d], rbuf.at[1 + d], res_s.at[1 + d], res_r.at[1 + d], (x + d, y))
+            part = pl.ds(middle * h, middle)
+            c = remote(
+                res.at[1 + d, part], rbuf.at[1 + d, part],
+                res_s.at[1 + d, h], res_r.at[1 + d, h], (x + d, y),
+            )
         c.wait_recv()
 
     def column(src, buf, send, recv):
@@ -124,6 +142,8 @@
     base = 4 * (x // 4)
     spot = lax.rem(x, 4)
 
+    loads[4].wait()
+    loads[5].wait()
     own = geo[...].astype(F32)
     own = jnp.concatenate([own, jnp.zeros((leaf_dev, 4, panels), F32)], axis=1)
     own = own.reshape(8 * leaf_dev, panels)
@@ -149,7 +169,7 @@
             sfeat[place * leaf_dev + k] = wide.T.astype(BF16)
             return carry
 
-        lax.fori_loop(0, leaf_dev, leaf, 0)
+        lax.fori_loop(0, leaf_dev, leaf, 0, unroll=4)
 
     def target_features(side, at):
         def leaf(l, carry):
@@ -165,7 +185,7 @@
                 tfeat[((side + 1) * leaf_dev + l) * 3 + dz + 1] = wide.astype(BF16)
             return carry
 
-        lax.fori_loop(0, leaf_dev, leaf, 0)
+        lax.fori_loop(0, leaf_dev, leaf, 0, unroll=4)
 
     def weights(side):
         mine = lists[side + 1]
@@ -173,7 +193,8 @@
         for s in range(3):
             for dz in (-1, 0, 1):
                 n = (x * n_gy + y + s - 1) * leaf_dev + dz + leaf
-                hits = jnp.where(mine == n, 1.0, 0.0)
+                there = jnp.logical_and(y + s >= 1, y + s <= n_gy)
+                hits = jnp.where(jnp.logical_and(mine == n, there), 1.0, 0.0)
                 count = jnp.sum(hits, axis=1, keepdims=True)
                 weight[((side + 1) * 3 + s) * 3 + dz + 1] = jnp.broadcast_to(
                     count, (leaf_dev, panels)
@@ -195,6 +216,11 @@
                 ).astype(BF16),
             )
 
+    source_features(1)
+    target_features(0, 1)
+    weights(0)
+    acc[...] = jnp.zeros_like(acc)
+
     loads[0].wait()
     loads[1].wait()
     parts = []
@@ -214,16 +240,21 @@
         @pl.when(has(d, y, n_gy))
         def _():
             geo_y(d).start()
-            src_y(d).start()
-
-    source_features(1)
-    target_features(0, 1)
-    weights(0)
-    acc[...] = jnp.zeros_like(acc)
+            src_y(d, 0).start()
+            src_y(d, 1).start()
+
+    lane = lax.broadcasted_iota(jnp.int32, (panels, FEATURES), 1)
+    away = jnp.where(lane == 3, 1.0, 0.0).astype(BF16)
     for d in sides:
         @pl.when(jnp.logical_not(has(d, x, n_gx)))
         def _():
             rbuf[1 + d] = jnp.zeros(rbuf.shape[1:], BF16)
+
+        @pl.when(jnp.logical_not(has(d, y, n_gy)))
+        def _():
+            hsrc[1 + d] = jnp.zeros(hsrc.shape[1:], BF16)
+            for k in range(leaf_dev):
+                sfeat[(1 + d) * leaf_dev + k] = away
 
     def coupled(level):
         c = coup[level]
@@ -296,6 +327,7 @@
         coarse = total([c3_buf[g] for g in range(4)])
         target[96:112, :] = coarse[:, 0:half]
         target[112:128, :] = coarse[:, half:]
+    def turn_bases():
         loads[3].wait()
 
         def take(k, b):
@@ -320,33 +352,61 @@
                 arrived(geo_y, d)
                 gf[1 + d] = gbuf[1 + d].astype(F32)
                 source_features(1 + d)
-                arrived(src_y, d)
-
-    def give(d):
-        @pl.when(has(d, x, n_gx))
-        def _():
-            res[1 + d] = acc[1 + d].astype(BF16)
-            res_x(d).start()
-
-    def chunk(s, t):
-        for l in range(leaf_dev):
-            ks = [k for k in (l - 1, l, l + 1) if 0 <= k < leaf_dev]
-            mats = []
-            for k in ks:
-                dz = k - l
+                arrived(src_y, d, 0)
+
+    def rest_of_column():
+        for d in sides:
+            @pl.when(has(d, y, n_gy))
+            def _():
+                arrived(src_y, d, 1)
+
+    def give(h):
+        for d in sides:
+            @pl.when(has(d, x, n_gx))
+            def _():
+                part = slice(middle * h, middle * h + middle)
+                res[1 + d, part] = acc[1 + d, part].astype(BF16)
+                res_x(d, h).start()
+
+    def chunk(t, halves):
+        work = [(s, h, i) for s, h in halves for i in range(middle)]
+
+        def leaves(h, i):
+            sign = 1 - 2 * h
+            l = (leaf_dev - 1) * h + sign * i
+            return l, [(l + sign * e, sign * e) for e in (-1, 0, 1) if i + e >= 0]
+
+        def fill(n):
+            s, h, i = work[n]
+            l, ks = leaves(h, i)
+            for at, (k, dz) in enumerate(ks):
                 squared = dot(sfeat[s * leaf_dev + k], tfeat[(t * leaf_dev + l) * 3 + dz + 1])
-                w = weight[(t * 3 + s) * 3 + dz + 1, l : l + 1, :]
-                mats.append((lax.rsqrt(squared) * w).astype(BF16))
-            wide = jnp.concatenate([hsrc[s, k] for k in ks], axis=1)
-            acc[t, l] += dot(wide, jnp.concatenate(mats, axis=0))
+                w = weight[(t * 3 + s) * 3 + dz + 1, pl.ds(l, 1), :]
+                mats[n % 2, panels * at : panels * (at + 1), :] = (
+                    lax.rsqrt(squared) * w
+                ).astype(BF16)
+
+        def apply(n):
+            s, h, i = work[n]
+            l, ks = leaves(h, i)
+            wide = jnp.concatenate([hsrc[s, k] for k, _ in ks], axis=1)
+            acc[t, l] += dot(wide, mats[n % 2, 0 : panels * len(ks), :])
+
+        fill(0)
+        for n in range(len(work)):
+            if n + 1 < len(work):
+                fill(n + 1)
+            apply(n)
 
     def step(c, carry):
         stages = {
             1: [from_row],
             2: [after_first],
-            3: [from_column, after_second],
-            5: [lambda: give(1), after_third],
-            7: [lambda: give(-1), after_fourth],
+            3: [from_column],
+            4: [after_second],
+            5: [lambda: give(0), rest_of_column],
+            7: [lambda: give(1), after_third],
+            8: [turn_bases],
         }
         for at, work in stages.items():
             @pl.when(c == at)
@@ -354,27 +414,28 @@
                 for one in work:
                     one()
 
-        s = jnp.where(c < 3, 1, 2 * lax.rem(c, 2))
-        late = jnp.where(c < 5, 2, jnp.where(c < 7, 0, 1))
-        t = jnp.where(c == 0, 1, jnp.where(c == 2, 0, late))
-        at_x, at_y = x + t - 1, y + s - 1
-        inside = jnp.logical_and(
-            jnp.logical_and(at_x >= 0, at_x < n_gx), jnp.logical_and(at_y >= 0, at_y < n_gy)
-        )
-
-        @pl.when(inside)
-        def _():
-            chunk(s, t)
+        own_turn = c < 3
+        t = jnp.where(jnp.logical_or(c == 0, c > 6), 1, 2 * lax.rem(c, 2))
+        half_turn = jnp.where(c < 7, (c - 3) // 2, c - 7)
+        a = (jnp.where(own_turn, 1, 2), jnp.where(own_turn, 0, half_turn))
+        b = (jnp.where(own_turn, 1, 0), jnp.where(own_turn, 1, half_turn))
+        at_x = x + t - 1
+
+        @pl.when(jnp.logical_and(at_x >= 0, at_x < n_gx))
+        def _():
+            chunk(t, [a, b])
 
         return carry
 
     lax.fori_loop(0, 9, step, 0)
 
+    after_fourth()
     turned = target[...].T.astype(BF16)
     for d in sides:
         @pl.when(has(d, x, n_gx))
         def _():
-            arrived(res_x, d)
+            arrived(res_x, d, 0)
+            arrived(res_x, d, 1)
     for k in range(leaf_dev):
         near_field = acc[1, k] + (rbuf[0, k].astype(F32) + rbuf[2, k].astype(F32))
         out[k] = near_field + dot(turned, by_leaf[k])
@@ -384,12 +445,14 @@
         def _():
             geo_x(d).wait_send()
             list_x(d).wait_send()
-            res_x(d).wait_send()
+            res_x(d, 0).wait_send()
+            res_x(d, 1).wait_send()
 
         @pl.when(has(d, y, n_gy))
         def _():
             geo_y(d).wait_send()
-            src_y(d).wait_send()
+            src_y(d, 0).wait_send()
+            src_y(d, 1).wait_send()
     for k in range(1, n_gy):
         to = lax.rem(y + k, n_gy)
         remote(proj, col_buf.at[y], p1_s.at[k], p1_r.at[y], (x, to)).wait_send()
@@ -413,11 +476,13 @@
         functools.partial(kernel, n_gx, n_gy),
         out_shape=jax.ShapeDtypeStruct((leaf_dev, rhs, panels), F32),
         in_specs=[
-            anywhere, vmem, vmem, pl.BlockSpec(memory_space=pltpu.SMEM),
+            anywhere, anywhere, anywhere, pl.BlockSpec(memory_space=pltpu.SMEM),
             anywhere, anywhere, anywhere,
         ],
         out_specs=vmem,
         scratch_shapes=[
+            pltpu.VMEM(geometry.shape[2:], BF16),
+            pltpu.VMEM(near_lists.shape[2:], jnp.int32),
             pltpu.VMEM((3, leaf_dev, rhs, panels), BF16),
             pltpu.VMEM((6, 8 * leaf_dev, panels), BF16),
             pltpu.VMEM((6, 8 * leaf_dev, panels), F32),
@@ -433,6 +498,7 @@
             pltpu.VMEM((panels // 128, flat_rows, 128), F32),
             pltpu.VMEM((leaf_dev, 128, panels), BF16),
             pltpu.VMEM(couplings.shape[2:], F32),
+            pltpu.VMEM((2, 3 * panels, panels), BF16),
             pltpu.VMEM((64, 2 * rhs), F32),
             pltpu.VMEM((n_gy, 64, 2 * rhs), F32),
             pltpu.VMEM((48, 2 * rhs), F32),
@@ -444,16 +510,16 @@
             pltpu.VMEM((16, 2 * rhs), F32),
             pltpu.VMEM((4, 16, 2 * rhs), F32),
             pltpu.VMEM((128, rhs), F32),
-            sems((4,)),
+            sems((6,)),
             sems((6,)), sems((6,)), sems((3,)), sems((3,)),
-            sems((3,)), sems((3,)), sems((3,)), sems((3,)),
+            sems((3, 2)), sems((3, 2)), sems((3, 2)), sems((3, 2)),
             sems((n_gy,)), sems((n_gy,)),
             sems((n_gx,)), sems((n_gx,)),
             sems((n_gy,)), sems((n_gy,)),
             sems((4,)), sems((4,)),
         ],
         compiler_params=pltpu.CompilerParams(
-            collective_id=0, has_side_effects=True, vmem_limit_bytes=40 * 1024 * 1024
+            collective_id=0, has_side_effects=True, vmem_limit_bytes=60 * 1024 * 1024
         ),
     )(
         sources[0, 0], geometry[0, 0], near_lists[0, 0], far_lists[0, 0],

time: 36.2 us -> 29.7 us (0.82)
  the two profiles are of different devices: /device:TPU:11 before, /device:TPU:1 now
where the time goes in v1:
time: 29.7 us; the launch traced here: 29.2 us
  Pallas kernels  27.3 us (92%)
  local copies, waits for them, and re-layouts  1.87 us (6%)
    pallas_call x1, Pallas kernels, body(): pl.pallas_call(functools.partial(kernel, n_gx, n_gy), out_shape=jax.Shape...  27.3 us
    unnamed x1, local copies, waits for them, and re-layouts  1.87 us

profile of v1, /device:TPU:1, one launch (start us, length us, event | category | flops | bytes accessed | tf_op | source)
XLA Modules:
  0.0 29.2 jit_solution(16036805001049011558)
XLA Ops:
  0.0 27.3 %shard_map.73 = f32[8,64,256]{2,1,0:T(8,128)} custom-call(bf16[8,64,256]{2,1,0:T(8,128)(2,1)} %bitcast.11, bf16[8,4,256]{2,1,0:T(4,128)(2,1)} %bitcast.13, s32[8,24]{1,0:T(8,128)} %bitcast.14, s32[4,16]{1,0:T(4,128)} %bitcast.15, bf16[1024,256]{1,0:T(8,128)(2,1)} %bitcast.9, bf16[1024,256]{1,0:T(8,128)(2,1)} %bitcast.10, f32[4,32,512]{2,1,0:T(8,128)} %bitcast.12), custom_call_target="tpu_custom_call" | custom-call | tf_op jit(solution)/shard_map/pallas_call | solution.py:475
  27.3 1.9 %copy.9 = f32[1,1,8,64,256]{4,3,2,1,0:T(8,128)} copy(f32[1,1,8,64,256]{4,3,2,1,0:T(8,128)} %bitcast.8) | data formatting | bytes 1048576

commit v2 on v1

--- a/solution.py
+++ b/solution.py
@@ -34,12 +34,13 @@
 
 
 def kernel(
-    n_gx, n_gy, src_in, geo_in, near_in, far, in_in, out_in, coup_in, out,
-    geo, near, hsrc, gbuf, gf, lists, weight, sfeat, tfeat, acc, res, rbuf,
-    base_in, base_out, flat, by_leaf, coup,
-    mats, proj, col_buf, row_src, row_buf, tab3, gath, int_src, int_buf, c3_src, c3_buf, target,
-    load, geo_s, geo_r, list_s, list_r, src_s, src_r, res_s, res_r,
-    p1_s, p1_r, p2_s, p2_r, p3_s, p3_r, p4_s, p4_r,
+    n_gx, n_gy, src_in, geo_in, near_in, far, in_in, out_in, coup_in, out, rbuf,
+    geo, near, hsrc, gbuf, gf, lists, weight, sfeat, tfeat, acc, res, zeros,
+    base_in, base_out, flat, by_leaf, target, coup, level0, level12, blocks, block_buf, group_src, group_buf,
+    mats, proj, col_buf, row_src, row_buf, tab3, int_src, int_buf,
+    load, out_s, fill_s, geo_s, geo_r, list_s, list_r, src_s, src_r, res_s, res_r,
+    p1_s, p1_r, p2_s, p2_r, p3_s, p3_r,
+    block_s, block_r, group_s, group_r,
 ):
     x = lax.axis_index("gx")
     y = lax.axis_index("gy")
@@ -60,7 +61,10 @@
     loads = [
         pltpu.make_async_copy(a, b, load.at[i])
         for i, (a, b) in enumerate(
-            [(src_in, hsrc.at[1]), (in_in, base_in), (coup_in, coup), (out_in, base_out), (geo_in, geo), (near_in, near)]
+            [
+                (src_in, hsrc.at[1]), (in_in, base_in), (coup_in, coup), (geo_in, geo), (near_in, near),
+                (out_in, base_out),
+            ]
         )
     ]
     for one in loads:
@@ -98,9 +102,15 @@
     def res_x(d, h):
         part = pl.ds(middle * h, middle)
         return remote(
-            res.at[1 + d, part], rbuf.at[1 - d, part],
+            res.at[1 + d, part], rbuf.at[(1 - d) // 2, part],
             res_s.at[1 + d, h], res_r.at[1 - d, h], (x + d, y),
         )
+
+    def absent(d):
+        return pltpu.make_async_copy(zeros, rbuf.at[(1 + d) // 2], fill_s.at[(1 + d) // 2])
+
+    def store(k):
+        return pltpu.make_async_copy(acc.at[1, k], out.at[k], out_s.at[k])
 
     def arrived(make, d, h=0):
         if make is geo_y:
@@ -120,7 +130,7 @@
         else:
             part = pl.ds(middle * h, middle)
             c = remote(
-                res.at[1 + d, part], rbuf.at[1 + d, part],
+                res.at[1 + d, part], rbuf.at[(1 + d) // 2, part],
                 res_s.at[1 + d, h], res_r.at[1 + d, h], (x + d, y),
             )
         c.wait_recv()
@@ -141,9 +151,55 @@
     half = rhs
     base = 4 * (x // 4)
     spot = lax.rem(x, 4)
-
+    mine = lax.rem(y, 4)
+    wide3 = 32 * (n_gx // 4)
+
+    loads[3].wait()
     loads[4].wait()
-    loads[5].wait()
+    def product(a, b):
+        a_high, b_high = a.astype(BF16), b.astype(BF16)
+        a_low = (a - a_high.astype(F32)).astype(BF16)
+        b_low = (b - b_high.astype(F32)).astype(BF16)
+        return dot(a_high, b_high) + (dot(a_low, b_high) + dot(a_high, b_low))
+
+    def by_cluster(level, clusters):
+        shape = (32, 32 * clusters)
+        lane = lax.broadcasted_iota(jnp.int32, shape, 1)
+        place = lane >> 5
+        same = (lane & 31) == lax.broadcasted_iota(jnp.int32, shape, 0)
+        pick = [
+            jnp.where(jnp.logical_and(same, place == far[level, m]), 1.0, 0.0).astype(BF16)
+            for m in range(16)
+        ]
+        split = jnp.concatenate(pieces(coup[level]), axis=0).astype(BF16)
+        v = dot(split, jnp.concatenate(pick, axis=0))
+        return (v[0:32] + v[32:64]) + v[64:96]
+
+    def block_copy(k):
+        to = lax.rem(y + k, n_gy)
+        return remote(
+            blocks.at[lax.rem(to, 4)], block_buf.at[y], block_s.at[k], block_r.at[y], (x, to)
+        )
+
+    def group_copy(k):
+        to = base + lax.rem(spot + k, 4)
+        return remote(group_src, group_buf.at[spot], group_s.at[k], group_r.at[spot], (to, y))
+
+    def gather_couplings():
+        v = by_cluster(3, n_gx // 4)
+        for b in range(4):
+            blocks[b, :, 0 : v.shape[1]] = v[8 * b : 8 * b + 8]
+
+    def give_couplings():
+        for k in range(1, n_gy):
+            block_copy(k).start()
+        block_buf[y] = blocks[mine]
+
+    def own_couplings():
+        level0[...] = by_cluster(0, n_gy)
+        level12[0:32, :] = by_cluster(1, n_gx)
+        level12[32:64, :] = by_cluster(2, n_gx)
+
     own = geo[...].astype(F32)
     own = jnp.concatenate([own, jnp.zeros((leaf_dev, 4, panels), F32)], axis=1)
     own = own.reshape(8 * leaf_dev, panels)
@@ -229,8 +285,11 @@
     proj[:, 0:half] = projection[0:64]
     proj[:, half:] = projection[64:128]
 
+    loads[2].wait()
+    gather_couplings()
     pl.semaphore_wait(barrier, n_gx - 1 + n_gy - 1)
     column(proj, col_buf, p1_s, p1_r)
+    give_couplings()
     for d in sides:
         @pl.when(has(d, x, n_gx))
         def _():
@@ -248,22 +307,14 @@
     for d in sides:
         @pl.when(jnp.logical_not(has(d, x, n_gx)))
         def _():
-            rbuf[1 + d] = jnp.zeros(rbuf.shape[1:], BF16)
+            zeros[...] = jnp.zeros(zeros.shape, BF16)
+            absent(d).start()
 
         @pl.when(jnp.logical_not(has(d, y, n_gy)))
         def _():
             hsrc[1 + d] = jnp.zeros(hsrc.shape[1:], BF16)
             for k in range(leaf_dev):
                 sfeat[(1 + d) * leaf_dev + k] = away
-
-    def coupled(level):
-        c = coup[level]
-        c_high = c.astype(BF16)
-        c_low = (c - c_high.astype(F32)).astype(BF16)
-        g = gath[...]
-        g_high = g.astype(BF16)
-        g_low = (g - g_high.astype(F32)).astype(BF16)
-        return dot(c_high, g_high) + (dot(c_low, g_high) + dot(c_high, g_low))
 
     def after_first():
         column_wait(proj, col_buf, p1_s, p1_r)
@@ -276,59 +327,49 @@
             to = lax.rem(x + k, n_gx)
             remote(row_src, row_buf.at[x], p2_s.at[k], p2_r.at[x], (to, y)).start()
         row_buf[x] = row_src[...]
-        loads[2].wait()
-        for m in range(16):
-            gath[pl.ds(m * 32, 32), :] = col_buf[far[0, m], 0:32, 0:half]
-        target[0:32, :] = coupled(0)
+        for k in range(1, n_gy):
+            peer = lax.rem(y + k, n_gy)
+            remote(
+                blocks.at[0], block_buf.at[peer], block_s.at[k], block_r.at[peer], (x, peer)
+            ).wait_recv()
+        group_src[:, 0:wide3] = total([block_buf[g, :, 0:wide3] for g in range(n_gy)])
+        for k in range(1, 4):
+            group_copy(k).start()
+        group_buf[spot] = group_src[...]
+        zero = jnp.concatenate([col_buf[g, 0:32, 0:half] for g in range(n_gy)], axis=0)
+        target[0:32, :] = product(level0[...], zero).astype(BF16)
 
     def after_second():
         for k in range(1, n_gx):
             peer = lax.rem(x + k, n_gx)
             remote(row_src, row_buf.at[peer], p2_s.at[k], p2_r.at[peer], (peer, y)).wait_recv()
-        for c in range(n_gx // 4):
-            coarse = total([row_buf[4 * c + g, 32:48, :] for g in range(4)])
-            tab3[c, 0:16, :] = coarse[:, 0:half]
-            tab3[c, 16:32, :] = coarse[:, half:]
-        for level in (1, 2, 3):
-            for m in range(16):
-                s = far[level, m]
-                if level == 3:
-                    gath[pl.ds(m * 32, 32), :] = tab3[s]
-                elif level == 1:
-                    gath[pl.ds(m * 32, 32), :] = row_buf[s, 0:32, 0:half]
-                else:
-                    gath[pl.ds(m * 32, 32), :] = row_buf[s, 0:32, half:]
-            term = coupled(level)
-            if level == 1:
-                int_src[0:32, 0:half] = term
-            elif level == 2:
-                int_src[0:32, half:] = term
-            else:
-                int_src[32:48, 0:half] = term[0:16]
-                int_src[32:48, half:] = term[16:32]
-        column(int_src, int_buf, p3_s, p3_r)
-
-    def after_third():
-        column_wait(int_src, int_buf, p3_s, p3_r)
-        c3_src[...] = total([int_buf[g, 32:48, :] for g in range(n_gy)])
-        for k in range(1, 4):
-            to = base + lax.rem(spot + k, 4)
-            remote(c3_src, c3_buf.at[spot], p4_s.at[k], p4_r.at[spot], (to, y)).start()
-        c3_buf[spot] = c3_src[...]
-        target[32:64, :] = total([int_buf[quarter + g, 0:32, 0:half] for g in range(4)])
-        target[64:96, :] = total([int_buf[g, 0:32, half:] for g in range(n_gy)])
-
-    def after_fourth():
         for k in range(1, 4):
             peer = lax.rem(spot + k, 4)
             remote(
-                c3_src, c3_buf.at[peer], p4_s.at[k], p4_r.at[peer], (base + peer, y)
+                group_src, group_buf.at[peer], group_s.at[k], group_r.at[peer], (base + peer, y)
             ).wait_recv()
-        coarse = total([c3_buf[g] for g in range(4)])
-        target[96:112, :] = coarse[:, 0:half]
-        target[112:128, :] = coarse[:, half:]
+        fine = jnp.concatenate([row_buf[g, 0:32] for g in range(n_gx)], axis=0)
+        both = product(level12[...], fine)
+        int_src[0:32, 0:half] = both[0:32, 0:half]
+        int_src[0:32, half:] = both[32:64, half:]
+        for c in range(n_gx // 4):
+            coarse = total([row_buf[4 * c + g, 32:48, :] for g in range(4)])
+            tab3[32 * c : 32 * c + 16, :] = coarse[:, 0:half]
+            tab3[32 * c + 16 : 32 * c + 32, :] = coarse[:, half:]
+        third = total([group_buf[g, :, 0:wide3] for g in range(4)])
+        int_src[32:40, 0:half] = product(third, tab3[...])
+        int_src[32:40, half:] = jnp.zeros((8, half), F32)
+        column(int_src, int_buf, p3_s, p3_r)
+
+    def after_third():
+        column_wait(int_src, int_buf, p3_s, p3_r)
+        target[32:64, :] = total([int_buf[quarter + g, 0:32, 0:half] for g in range(4)]).astype(BF16)
+        target[64:96, :] = total([int_buf[g, 0:32, half:] for g in range(n_gy)]).astype(BF16)
+        third = [int_buf[quarter + b, 32:40, 0:half] for b in range(4)]
+        target[96:128, :] = jnp.concatenate(third, axis=0).astype(BF16)
+
     def turn_bases():
-        loads[3].wait()
+        loads[5].wait()
 
         def take(k, b):
             by_leaf[k] = b
@@ -397,6 +438,8 @@
             if n + 1 < len(work):
                 fill(n + 1)
             apply(n)
+
+    own_couplings()
 
     def step(c, carry):
         stages = {
@@ -429,16 +472,21 @@
 
     lax.fori_loop(0, 9, step, 0)
 
-    after_fourth()
-    turned = target[...].T.astype(BF16)
+    turned = target[...].astype(F32).T.astype(BF16)
+    for k in range(leaf_dev):
+        acc[1, k] += dot(turned, by_leaf[k])
+        store(k).start()
     for d in sides:
         @pl.when(has(d, x, n_gx))
         def _():
             arrived(res_x, d, 0)
             arrived(res_x, d, 1)
+
+        @pl.when(jnp.logical_not(has(d, x, n_gx)))
+        def _():
+            absent(d).wait()
     for k in range(leaf_dev):
-        near_field = acc[1, k] + (rbuf[0, k].astype(F32) + rbuf[2, k].astype(F32))
-        out[k] = near_field + dot(turned, by_leaf[k])
+        store(k).wait()
 
     for d in sides:
         @pl.when(has(d, x, n_gx))
@@ -457,29 +505,31 @@
         to = lax.rem(y + k, n_gy)
         remote(proj, col_buf.at[y], p1_s.at[k], p1_r.at[y], (x, to)).wait_send()
         remote(int_src, int_buf.at[y], p3_s.at[k], p3_r.at[y], (x, to)).wait_send()
+        block_copy(k).wait_send()
+    for k in range(1, 4):
+        group_copy(k).wait_send()
     for k in range(1, n_gx):
         to = lax.rem(x + k, n_gx)
         remote(row_src, row_buf.at[x], p2_s.at[k], p2_r.at[x], (to, y)).wait_send()
-    for k in range(1, 4):
-        to = base + lax.rem(spot + k, 4)
-        remote(c3_src, c3_buf.at[spot], p4_s.at[k], p4_r.at[spot], (to, y)).wait_send()
 
 
 def body(sources, geometry, near_lists, far_lists, bases_in, bases_out, couplings):
     leaf_dev, rhs, panels = sources.shape[2:]
     n_gx, n_gy = lax.axis_size("gx"), lax.axis_size("gy")
-    vmem = pl.BlockSpec(memory_space=pltpu.VMEM)
-    anywhere = pl.BlockSpec(memory_space=pl.ANY)
+    anywhere = pl.BlockSpec(memory_space=pltpu.HBM)
     sems = pltpu.SemaphoreType.DMA
     flat_rows = bases_in.shape[2] * bases_in.shape[3] * leaf_dev
-    potential = pl.pallas_call(
+    own, given = pl.pallas_call(
         functools.partial(kernel, n_gx, n_gy),
-        out_shape=jax.ShapeDtypeStruct((leaf_dev, rhs, panels), F32),
+        out_shape=(
+            jax.ShapeDtypeStruct((leaf_dev, rhs, panels), F32),
+            jax.ShapeDtypeStruct((2, leaf_dev, rhs, panels), BF16),
+        ),
         in_specs=[
             anywhere, anywhere, anywhere, pl.BlockSpec(memory_space=pltpu.SMEM),
             anywhere, anywhere, anywhere,
         ],
-        out_specs=vmem,
+        out_specs=(anywhere, anywhere),
         scratch_shapes=[
             pltpu.VMEM(geometry.shape[2:], BF16),
             pltpu.VMEM(near_lists.shape[2:], jnp.int32),
@@ -492,40 +542,45 @@
             pltpu.VMEM((9 * leaf_dev, FEATURES, panels), BF16),
             pltpu.VMEM((3, leaf_dev, rhs, panels), F32),
             pltpu.VMEM((3, leaf_dev, rhs, panels), BF16),
-            pltpu.VMEM((3, leaf_dev, rhs, panels), BF16),
+            pltpu.VMEM((leaf_dev, rhs, panels), BF16),
             pltpu.VMEM((flat_rows, panels), BF16),
             pltpu.VMEM((flat_rows, panels), BF16),
             pltpu.VMEM((panels // 128, flat_rows, 128), F32),
             pltpu.VMEM((leaf_dev, 128, panels), BF16),
+            pltpu.VMEM((128, rhs), BF16),
             pltpu.VMEM(couplings.shape[2:], F32),
+            pltpu.VMEM((32, 32 * n_gy), F32),
+            pltpu.VMEM((64, 32 * n_gx), F32),
+            pltpu.VMEM((4, 8, max(128, 8 * n_gx)), F32),
+            pltpu.VMEM((n_gy, 8, max(128, 8 * n_gx)), F32),
+            pltpu.VMEM((8, max(128, 8 * n_gx)), F32),
+            pltpu.VMEM((4, 8, max(128, 8 * n_gx)), F32),
             pltpu.VMEM((2, 3 * panels, panels), BF16),
             pltpu.VMEM((64, 2 * rhs), F32),
             pltpu.VMEM((n_gy, 64, 2 * rhs), F32),
             pltpu.VMEM((48, 2 * rhs), F32),
             pltpu.VMEM((n_gx, 48, 2 * rhs), F32),
-            pltpu.VMEM((n_gx // 4, 32, rhs), F32),
-            pltpu.VMEM((512, rhs), F32),
-            pltpu.VMEM((48, 2 * rhs), F32),
-            pltpu.VMEM((n_gy, 48, 2 * rhs), F32),
-            pltpu.VMEM((16, 2 * rhs), F32),
-            pltpu.VMEM((4, 16, 2 * rhs), F32),
-            pltpu.VMEM((128, rhs), F32),
-            sems((6,)),
+            pltpu.VMEM((8 * n_gx, rhs), F32),
+            pltpu.VMEM((40, 2 * rhs), F32),
+            pltpu.VMEM((n_gy, 40, 2 * rhs), F32),
+            sems((6,)), sems((leaf_dev,)), sems((2,)),
             sems((6,)), sems((6,)), sems((3,)), sems((3,)),
             sems((3, 2)), sems((3, 2)), sems((3, 2)), sems((3, 2)),
             sems((n_gy,)), sems((n_gy,)),
             sems((n_gx,)), sems((n_gx,)),
             sems((n_gy,)), sems((n_gy,)),
+            sems((n_gy,)), sems((n_gy,)),
             sems((4,)), sems((4,)),
         ],
         compiler_params=pltpu.CompilerParams(
-            collective_id=0, has_side_effects=True, vmem_limit_bytes=60 * 1024 * 1024
+            collective_id=0, has_side_effects=True, vmem_limit_bytes=61440 * 1024
         ),
     )(
         sources[0, 0], geometry[0, 0], near_lists[0, 0], far_lists[0, 0],
         bases_in.reshape(flat_rows, panels), bases_out.reshape(flat_rows, panels),
         couplings[0, 0],
     )
+    potential = own + (given[0].astype(F32) + given[1].astype(F32))
     return potential.reshape(sources.shape)
 
 

time: 29.7 us -> 27.9 us (0.939); the launches traced: 29.2 us -> 27.8 us
  other arithmetic: 0 us -> 2.06 us
  local copies, waits for them, and re-layouts: 1.87 us -> 0 us
  Pallas kernels: 27.3 us -> 25.7 us
    reshape x0 -> x1, other arithmetic: none -> 2.06 us  [body(): return potential.reshape(sources.shape)]
    unnamed x1 -> x0, local copies, waits for them, and re-layouts: 1.87 us -> none
    pallas_call x1, Pallas kernels: 27.3 us -> 25.7 us  [body(): pl.pallas_call(functools.partial(kernel, n_gx, n_gy), out_shape=(jax.Shap...]
where the time goes in v2:
time: 27.9 us; the launch traced here: 27.8 us
  Pallas kernels  25.7 us (92%)
  other arithmetic  2.06 us (7%)
    pallas_call x1, Pallas kernels, body(): pl.pallas_call(functools.partial(kernel, n_gx, n_gy), out_shape=(jax.Shap...  25.7 us
    reshape x1, other arithmetic, body(): return potential.reshape(sources.shape)  2.06 us

profile of v2, /device:TPU:1, one launch (start us, length us, event | category | flops | bytes accessed | tf_op | source)
XLA Modules:
  0.0 27.8 jit_solution(3757440850133843727)
XLA Ops:
  0.0 25.7 %shard_map.73 = (f32[8,64,256]{2,1,0:T(8,128)}, bf16[2,8,64,256]{3,2,1,0:T(8,128)(2,1)}) custom-call(bf16[8,64,256]{2,1,0:T(8,128)(2,1)} %bitcast.15, bf16[8,4,256]{2,1,0:T(4,128)(2,1)} %bitcast.17, s32[8,24]{1,0:T(8,128)} %bitcast.18, s32[4,16]{1,0:T(4,128)} %bitcast.19, bf16[1024,256]{1,0:T(8,128)(2,1)} %bitcast.13, bf16[1024,256]{1,0:T(8,128)(2,1)} %bitcast.14, ...), custom_call_target="tpu_custom_call" | custom-call | tf_op jit(solution)/shard_map/pallas_call | solution.py:522
  25.7 2.1 %fusion = f32[1,1,8,64,256]{4,3,2,1,0:T(8,128)} fusion(f32[8,64,256]{2,1,0:T(8,128)} %get-tuple-element.7, bf16[2,8,64,256]{3,2,1,0:T(8,128)(2,1)} %get-tuple-element.8), kind=kLoop, calls=%fused_computation.1 | loop fusion | flops 524288 | bytes 1572864 | tf_op jit(solution)/shard_map/reshape | solution.py:584

commit v3 on v2

--- a/solution.py
+++ b/solution.py
@@ -35,7 +35,7 @@
 
 def kernel(
     n_gx, n_gy, src_in, geo_in, near_in, far, in_in, out_in, coup_in, out, rbuf,
-    geo, near, hsrc, gbuf, gf, lists, weight, sfeat, tfeat, acc, res, zeros,
+    hsrc, gbuf, gf, lists, weight, sfeat, tfeat, acc, res, zeros,
     base_in, base_out, flat, by_leaf, target, coup, level0, level12, blocks, block_buf, group_src, group_buf,
     mats, proj, col_buf, row_src, row_buf, tab3, int_src, int_buf,
     load, out_s, fill_s, geo_s, geo_r, list_s, list_r, src_s, src_r, res_s, res_r,
@@ -45,7 +45,6 @@
     x = lax.axis_index("gx")
     y = lax.axis_index("gy")
     leaf_dev, rhs, panels = out.shape
-    slots = near.shape[1]
     middle = leaf_dev // 2
     first = middle + 1
     barrier = pltpu.get_barrier_semaphore()
@@ -62,7 +61,7 @@
         pltpu.make_async_copy(a, b, load.at[i])
         for i, (a, b) in enumerate(
             [
-                (src_in, hsrc.at[1]), (in_in, base_in), (coup_in, coup), (geo_in, geo), (near_in, near),
+                (src_in, hsrc.at[1]), (in_in, base_in), (coup_in, coup), (geo_in, gbuf.at[1]), (near_in, lists.at[1]),
                 (out_in, base_out),
             ]
         )
@@ -82,20 +81,20 @@
     sides = (-1, 1)
 
     def geo_y(d):
-        return remote(gbuf.at[1], gbuf.at[1 - d], geo_s.at[1 + d], geo_r.at[1 - d], (x, y + d))
+        return remote(geo_in, gbuf.at[1 - d], geo_s.at[1 + d], geo_r.at[1 - d], (x, y + d))
 
     def geo_x(d):
         return remote(
-            gbuf.at[1], gbuf.at[4 - d], geo_s.at[4 + d], geo_r.at[4 - d], (x + d, y)
+            geo_in, gbuf.at[4 - d], geo_s.at[4 + d], geo_r.at[4 - d], (x + d, y)
         )
 
     def list_x(d):
-        return remote(lists.at[1], lists.at[1 - d], list_s.at[1 + d], list_r.at[1 - d], (x + d, y))
+        return remote(near_in, lists.at[1 - d], list_s.at[1 + d], list_r.at[1 - d], (x + d, y))
 
     def src_y(d, h):
         part = pl.ds(first * h, first if h == 0 else leaf_dev - first)
         return remote(
-            hsrc.at[1, part], hsrc.at[1 - d, part],
+            src_in.at[part], hsrc.at[1 - d, part],
             src_s.at[1 + d, h], src_r.at[1 - d, h], (x, y + d),
         )
 
@@ -154,8 +153,6 @@
     mine = lax.rem(y, 4)
     wide3 = 32 * (n_gx // 4)
 
-    loads[3].wait()
-    loads[4].wait()
     def product(a, b):
         a_high, b_high = a.astype(BF16), b.astype(BF16)
         a_low = (a - a_high.astype(F32)).astype(BF16)
@@ -200,13 +197,10 @@
         level12[0:32, :] = by_cluster(1, n_gx)
         level12[32:64, :] = by_cluster(2, n_gx)
 
-    own = geo[...].astype(F32)
-    own = jnp.concatenate([own, jnp.zeros((leaf_dev, 4, panels), F32)], axis=1)
-    own = own.reshape(8 * leaf_dev, panels)
-    gbuf[1] = own.astype(BF16)
-    gf[1] = own
-    lists[1] = jnp.full(lists.shape[1:], -1, jnp.int32)
-    lists[1, :, 0:slots] = near[...]
+    def spread(at):
+        raw = gbuf[at].astype(F32)
+        raw = jnp.concatenate([raw, jnp.zeros((leaf_dev, 4, panels), F32)], axis=1)
+        gf[at] = raw.reshape(8 * leaf_dev, panels)
 
     def source_features(place):
         shift = lax.convert_element_type(place - 1, F32)
@@ -272,36 +266,60 @@
                 ).astype(BF16),
             )
 
-    source_features(1)
-    target_features(0, 1)
-    weights(0)
-    acc[...] = jnp.zeros_like(acc)
-
-    loads[0].wait()
-    loads[1].wait()
-    parts = []
-    transposed(base_in, lambda k, b: parts.append(dot(b, hsrc[1, k], 1, 1)))
-    projection = total(parts)
-    proj[:, 0:half] = projection[0:64]
-    proj[:, half:] = projection[64:128]
-
-    loads[2].wait()
-    gather_couplings()
-    pl.semaphore_wait(barrier, n_gx - 1 + n_gy - 1)
-    column(proj, col_buf, p1_s, p1_r)
+    def projections():
+        loads[0].wait()
+        loads[1].wait()
+        parts = []
+        transposed(base_in, lambda k, b: parts.append(dot(b, hsrc[1, k], 1, 1)))
+        projection = total(parts)
+        proj[:, 0:half] = projection[0:64]
+        proj[:, half:] = projection[64:128]
+
+    def own_features():
+        loads[3].wait()
+        loads[4].wait()
+        spread(1)
+        source_features(1)
+        target_features(0, 1)
+        weights(0)
+        acc[...] = jnp.zeros_like(acc)
+
+    def couplings():
+        loads[2].wait()
+        gather_couplings()
+
+    def enter():
+        pl.semaphore_wait(barrier, n_gx - 1 + n_gy - 1)
+
+    def send_geometry():
+        for d in sides:
+            @pl.when(has(d, x, n_gx))
+            def _():
+                geo_x(d).start()
+                list_x(d).start()
+
+            @pl.when(has(d, y, n_gy))
+            def _():
+                geo_y(d).start()
+
+    def send_sources():
+        for d in sides:
+            @pl.when(has(d, y, n_gy))
+            def _():
+                src_y(d, 0).start()
+                src_y(d, 1).start()
+
+    def send_projections():
+        column(proj, col_buf, p1_s, p1_r)
+
+    projections()
+    enter()
+    send_geometry()
+    send_projections()
+    couplings()
     give_couplings()
-    for d in sides:
-        @pl.when(has(d, x, n_gx))
-        def _():
-            geo_x(d).start()
-            list_x(d).start()
-
-        @pl.when(has(d, y, n_gy))
-        def _():
-            geo_y(d).start()
-            src_y(d, 0).start()
-            src_y(d, 1).start()
-
+    send_sources()
+    own_features()
     lane = lax.broadcasted_iota(jnp.int32, (panels, FEATURES), 1)
     away = jnp.where(lane == 3, 1.0, 0.0).astype(BF16)
     for d in sides:
@@ -382,7 +400,7 @@
             def _():
                 arrived(geo_x, d)
                 arrived(list_x, d)
-                gf[4 + d] = gbuf[4 + d].astype(F32)
+                spread(4 + d)
                 target_features(d, 4 + d)
                 weights(d)
 
@@ -391,7 +409,7 @@
             @pl.when(has(d, y, n_gy))
             def _():
                 arrived(geo_y, d)
-                gf[1 + d] = gbuf[1 + d].astype(F32)
+                spread(1 + d)
                 source_features(1 + d)
                 arrived(src_y, d, 0)
 
@@ -401,13 +419,14 @@
             def _():
                 arrived(src_y, d, 1)
 
-    def give(h):
-        for d in sides:
-            @pl.when(has(d, x, n_gx))
-            def _():
-                part = slice(middle * h, middle * h + middle)
-                res[1 + d, part] = acc[1 + d, part].astype(BF16)
-                res_x(d, h).start()
+    outer = 2 * lax.rem(x, 2)
+
+    def give(t, h):
+        @pl.when(jnp.logical_and(x + t >= 1, x + t <= n_gx))
+        def _():
+            part = pl.ds(middle * h, middle)
+            res[t, part] = acc[t, part].astype(BF16)
+            res_x(t - 1, h).start()
 
     def chunk(t, halves):
         work = [(s, h, i) for s, h in halves for i in range(middle)]
@@ -445,11 +464,12 @@
         stages = {
             1: [from_row],
             2: [after_first],
-            3: [from_column],
-            4: [after_second],
-            5: [lambda: give(0), rest_of_column],
-            7: [lambda: give(1), after_third],
-            8: [turn_bases],
+            3: [turn_bases, from_column],
+            4: [lambda: give(outer, 0), after_second, rest_of_column],
+            5: [lambda: give(outer, 1)],
+            6: [lambda: give(2 - outer, 0)],
+            7: [lambda: give(2 - outer, 1)],
+
         }
         for at, work in stages.items():
             @pl.when(c == at)
@@ -458,8 +478,9 @@
                     one()
 
         own_turn = c < 3
-        t = jnp.where(jnp.logical_or(c == 0, c > 6), 1, 2 * lax.rem(c, 2))
-        half_turn = jnp.where(c < 7, (c - 3) // 2, c - 7)
+        other = jnp.where(jnp.logical_or(c == 1, jnp.logical_or(c == 3, c == 4)), outer, 2 - outer)
+        t = jnp.where(jnp.logical_or(c == 0, c > 6), 1, other)
+        half_turn = lax.rem(c + 1, 2)
         a = (jnp.where(own_turn, 1, 2), jnp.where(own_turn, 0, half_turn))
         b = (jnp.where(own_turn, 1, 0), jnp.where(own_turn, 1, half_turn))
         at_x = x + t - 1
@@ -472,6 +493,7 @@
 
     lax.fori_loop(0, 9, step, 0)
 
+    after_third()
     turned = target[...].astype(F32).T.astype(BF16)
     for k in range(leaf_dev):
         acc[1, k] += dot(turned, by_leaf[k])
@@ -531,12 +553,10 @@
         ],
         out_specs=(anywhere, anywhere),
         scratch_shapes=[
-            pltpu.VMEM(geometry.shape[2:], BF16),
-            pltpu.VMEM(near_lists.shape[2:], jnp.int32),
             pltpu.VMEM((3, leaf_dev, rhs, panels), BF16),
-            pltpu.VMEM((6, 8 * leaf_dev, panels), BF16),
+            pltpu.VMEM((6,) + geometry.shape[2:], BF16),
             pltpu.VMEM((6, 8 * leaf_dev, panels), F32),
-            pltpu.VMEM((3, leaf_dev, 128), jnp.int32),
+            pltpu.VMEM((3,) + near_lists.shape[2:], jnp.int32),
             pltpu.VMEM((27, leaf_dev, panels), F32),
             pltpu.VMEM((3 * leaf_dev, panels, FEATURES), BF16),
             pltpu.VMEM((9 * leaf_dev, FEATURES, panels), BF16),

time: 27.9 us -> 27.2 us (0.975)
  Pallas kernels: 25.7 us -> 24.9 us
    pallas_call x1, Pallas kernels: 25.7 us -> 24.9 us  [body(): pl.pallas_call(functools.partial(kernel, n_gx, n_gy), out_shape=(jax.Shap...]
where the time goes in v3:
time: 27.2 us; the launch traced here: 27 us
  Pallas kernels  24.9 us (92%)
  other arithmetic  2.06 us (8%)
    pallas_call x1, Pallas kernels, body(): pl.pallas_call(functools.partial(kernel, n_gx, n_gy), out_shape=(jax.Shap...  24.9 us
    reshape x1, other arithmetic, body(): return potential.reshape(sources.shape)  2.06 us

profile of v3, /device:TPU:1, one launch (start us, length us, event | category | flops | bytes accessed | tf_op | source)
XLA Modules:
  0.0 27.0 jit_solution(14941399343967024475)
XLA Ops:
  0.0 24.9 %shard_map.73 = (f32[8,64,256]{2,1,0:T(8,128)}, bf16[2,8,64,256]{3,2,1,0:T(8,128)(2,1)}) custom-call(bf16[8,64,256]{2,1,0:T(8,128)(2,1)} %bitcast.15, bf16[8,4,256]{2,1,0:T(4,128)(2,1)} %bitcast.17, s32[8,24]{1,0:T(8,128)} %bitcast.18, s32[4,16]{1,0:T(4,128)} %bitcast.19, bf16[1024,256]{1,0:T(8,128)(2,1)} %bitcast.13, bf16[1024,256]{1,0:T(8,128)(2,1)} %bitcast.14, ...), custom_call_target="tpu_custom_call" | custom-call | tf_op jit(solution)/shard_map/pallas_call | solution.py:544
  25.0 2.1 %fusion = f32[1,1,8,64,256]{4,3,2,1,0:T(8,128)} fusion(f32[8,64,256]{2,1,0:T(8,128)} %get-tuple-element.7, bf16[2,8,64,256]{3,2,1,0:T(8,128)(2,1)} %get-tuple-element.8), kind=kLoop, calls=%fused_computation.1 | loop fusion | flops 524288 | bytes 1572864 | tf_op jit(solution)/shard_map/reshape | solution.py:604

commit v4 on v3

--- a/solution.py
+++ b/solution.py
@@ -68,6 +68,7 @@
     ]
     for one in loads:
         one.start()
+    acc[...] = jnp.zeros_like(acc)
 
     def remote(src, dst, send, recv, where):
         return pltpu.make_async_remote_copy(
@@ -219,7 +220,7 @@
             sfeat[place * leaf_dev + k] = wide.T.astype(BF16)
             return carry
 
-        lax.fori_loop(0, leaf_dev, leaf, 0, unroll=4)
+        lax.fori_loop(0, leaf_dev, leaf, 0, unroll=8)
 
     def target_features(side, at):
         def leaf(l, carry):
@@ -235,7 +236,7 @@
                 tfeat[((side + 1) * leaf_dev + l) * 3 + dz + 1] = wide.astype(BF16)
             return carry
 
-        lax.fori_loop(0, leaf_dev, leaf, 0, unroll=4)
+        lax.fori_loop(0, leaf_dev, leaf, 0, unroll=8)
 
     def weights(side):
         mine = lists[side + 1]
@@ -282,7 +283,6 @@
         source_features(1)
         target_features(0, 1)
         weights(0)
-        acc[...] = jnp.zeros_like(acc)
 
     def couplings():
         loads[2].wait()
@@ -465,9 +465,9 @@
             1: [from_row],
             2: [after_first],
             3: [turn_bases, from_column],
-            4: [lambda: give(outer, 0), after_second, rest_of_column],
-            5: [lambda: give(outer, 1)],
-            6: [lambda: give(2 - outer, 0)],
+            4: [lambda: give(outer, 0)],
+            5: [lambda: give(2 - outer, 0), rest_of_column, after_second],
+            6: [lambda: give(outer, 1)],
             7: [lambda: give(2 - outer, 1)],
 
         }
@@ -478,9 +478,9 @@
                     one()
 
         own_turn = c < 3
-        other = jnp.where(jnp.logical_or(c == 1, jnp.logical_or(c == 3, c == 4)), outer, 2 - outer)
+        other = jnp.where(lax.rem(c, 2) == 1, outer, 2 - outer)
         t = jnp.where(jnp.logical_or(c == 0, c > 6), 1, other)
-        half_turn = lax.rem(c + 1, 2)
+        half_turn = jnp.where(c < 7, (c - 3) // 2, c - 7)
         a = (jnp.where(own_turn, 1, 2), jnp.where(own_turn, 0, half_turn))
         b = (jnp.where(own_turn, 1, 0), jnp.where(own_turn, 1, half_turn))
         at_x = x + t - 1

time: 27.2 us -> 26.3 us (0.967)
  Pallas kernels: 24.9 us -> 24 us
    pallas_call x1, Pallas kernels: 24.9 us -> 24 us  [body(): pl.pallas_call(functools.partial(kernel, n_gx, n_gy), out_shape=(jax.Shap...]
where the time goes in v4:
time: 26.3 us; the launch traced here: 26 us
  Pallas kernels  24 us (91%)
  other arithmetic  2.06 us (8%)
    pallas_call x1, Pallas kernels, body(): pl.pallas_call(functools.partial(kernel, n_gx, n_gy), out_shape=(jax.Shap...  24 us
    reshape x1, other arithmetic, body(): return potential.reshape(sources.shape)  2.06 us

profile of v4, /device:TPU:1, one launch (start us, length us, event | category | flops | bytes accessed | tf_op | source)
XLA Modules:
  0.0 26.0 jit_solution(13259901374890552312)
XLA Ops:
  0.0 24.0 %shard_map.73 = (f32[8,64,256]{2,1,0:T(8,128)}, bf16[2,8,64,256]{3,2,1,0:T(8,128)(2,1)}) custom-call(bf16[8,64,256]{2,1,0:T(8,128)(2,1)} %bitcast.15, bf16[8,4,256]{2,1,0:T(4,128)(2,1)} %bitcast.17, s32[8,24]{1,0:T(8,128)} %bitcast.18, s32[4,16]{1,0:T(4,128)} %bitcast.19, bf16[1024,256]{1,0:T(8,128)(2,1)} %bitcast.13, bf16[1024,256]{1,0:T(8,128)(2,1)} %bitcast.14, ...), custom_call_target="tpu_custom_call" | custom-call | tf_op jit(solution)/shard_map/pallas_call | solution.py:544
  24.0 2.1 %fusion = f32[1,1,8,64,256]{4,3,2,1,0:T(8,128)} fusion(f32[8,64,256]{2,1,0:T(8,128)} %get-tuple-element.7, bf16[2,8,64,256]{3,2,1,0:T(8,128)(2,1)} %get-tuple-element.8), kind=kLoop, calls=%fused_computation.1 | loop fusion | flops 524288 | bytes 1572864 | tf_op jit(solution)/shard_map/reshape | solution.py:604

commit v5 on v4

--- a/solution.py
+++ b/solution.py
@@ -466,8 +466,8 @@
             2: [after_first],
             3: [turn_bases, from_column],
             4: [lambda: give(outer, 0)],
-            5: [lambda: give(2 - outer, 0), rest_of_column, after_second],
-            6: [lambda: give(outer, 1)],
+            5: [lambda: give(2 - outer, 0), rest_of_column],
+            6: [after_second, lambda: give(outer, 1)],
             7: [lambda: give(2 - outer, 1)],
 
         }

time: 26.3 us -> 26.3 us (level)
  no operation moved by 1% of the time
where the time goes in v5:
time: 26.3 us; the launch traced here: 26.1 us
  Pallas kernels  24 us (91%)
  other arithmetic  2.06 us (8%)
    pallas_call x1, Pallas kernels, body(): pl.pallas_call(functools.partial(kernel, n_gx, n_gy), out_shape=(jax.Shap...  24 us
    reshape x1, other arithmetic, body(): return potential.reshape(sources.shape)  2.06 us

profile of v5, /device:TPU:1, one launch (start us, length us, event | category | flops | bytes accessed | tf_op | source)
XLA Modules:
  0.0 26.1 jit_solution(1113606426235221289)
XLA Ops:
  0.0 24.0 %shard_map.73 = (f32[8,64,256]{2,1,0:T(8,128)}, bf16[2,8,64,256]{3,2,1,0:T(8,128)(2,1)}) custom-call(bf16[8,64,256]{2,1,0:T(8,128)(2,1)} %bitcast.15, bf16[8,4,256]{2,1,0:T(4,128)(2,1)} %bitcast.17, s32[8,24]{1,0:T(8,128)} %bitcast.18, s32[4,16]{1,0:T(4,128)} %bitcast.19, bf16[1024,256]{1,0:T(8,128)(2,1)} %bitcast.13, bf16[1024,256]{1,0:T(8,128)(2,1)} %bitcast.14, ...), custom_call_target="tpu_custom_call" | custom-call | tf_op jit(solution)/shard_map/pallas_call | solution.py:544
  24.0 2.1 %fusion = f32[1,1,8,64,256]{4,3,2,1,0:T(8,128)} fusion(f32[8,64,256]{2,1,0:T(8,128)} %get-tuple-element.7, bf16[2,8,64,256]{3,2,1,0:T(8,128)(2,1)} %get-tuple-element.8), kind=kLoop, calls=%fused_computation.1 | loop fusion | flops 524288 | bytes 1572864 | tf_op jit(solution)/shard_map/reshape | solution.py:604

commit v6 on v4

--- a/solution.py
+++ b/solution.py
@@ -302,12 +302,11 @@
             def _():
                 geo_y(d).start()
 
-    def send_sources():
+    def send_sources(h):
         for d in sides:
             @pl.when(has(d, y, n_gy))
             def _():
-                src_y(d, 0).start()
-                src_y(d, 1).start()
+                src_y(d, h).start()
 
     def send_projections():
         column(proj, col_buf, p1_s, p1_r)
@@ -318,7 +317,7 @@
     send_projections()
     couplings()
     give_couplings()
-    send_sources()
+    send_sources(0)
     own_features()
     lane = lax.broadcasted_iota(jnp.int32, (panels, FEATURES), 1)
     away = jnp.where(lane == 3, 1.0, 0.0).astype(BF16)
@@ -463,7 +462,7 @@
     def step(c, carry):
         stages = {
             1: [from_row],
-            2: [after_first],
+            2: [after_first, lambda: send_sources(1)],
             3: [turn_bases, from_column],
             4: [lambda: give(outer, 0)],
             5: [lambda: give(2 - outer, 0), rest_of_column, after_second],

time: 26.3 us -> 26.3 us (level)
  no operation moved by 1% of the time
where the time goes in v6:
time: 26.3 us; the launch traced here: 26.1 us
  Pallas kernels  24 us (91%)
  other arithmetic  2.06 us (8%)
    pallas_call x1, Pallas kernels, body(): pl.pallas_call(functools.partial(kernel, n_gx, n_gy), out_shape=(jax.Shap...  24 us
    reshape x1, other arithmetic, body(): return potential.reshape(sources.shape)  2.06 us

profile of v6, /device:TPU:1, one launch (start us, length us, event | category | flops | bytes accessed | tf_op | source)
XLA Modules:
  0.0 26.1 jit_solution(892290847062509318)
XLA Ops:
  0.0 24.0 %shard_map.73 = (f32[8,64,256]{2,1,0:T(8,128)}, bf16[2,8,64,256]{3,2,1,0:T(8,128)(2,1)}) custom-call(bf16[8,64,256]{2,1,0:T(8,128)(2,1)} %bitcast.15, bf16[8,4,256]{2,1,0:T(4,128)(2,1)} %bitcast.17, s32[8,24]{1,0:T(8,128)} %bitcast.18, s32[4,16]{1,0:T(4,128)} %bitcast.19, bf16[1024,256]{1,0:T(8,128)(2,1)} %bitcast.13, bf16[1024,256]{1,0:T(8,128)(2,1)} %bitcast.14, ...), custom_call_target="tpu_custom_call" | custom-call | tf_op jit(solution)/shard_map/pallas_call | solution.py:543
  24.0 2.1 %fusion = f32[1,1,8,64,256]{4,3,2,1,0:T(8,128)} fusion(f32[8,64,256]{2,1,0:T(8,128)} %get-tuple-element.7, bf16[2,8,64,256]{3,2,1,0:T(8,128)(2,1)} %get-tuple-element.8), kind=kLoop, calls=%fused_computation.1 | loop fusion | flops 524288 | bytes 1572864 | tf_op jit(solution)/shard_map/reshape | solution.py:603

commit v7 on v4

--- a/solution.py
+++ b/solution.py
@@ -442,7 +442,7 @@
             for at, (k, dz) in enumerate(ks):
                 squared = dot(sfeat[s * leaf_dev + k], tfeat[(t * leaf_dev + l) * 3 + dz + 1])
                 w = weight[(t * 3 + s) * 3 + dz + 1, pl.ds(l, 1), :]
-                mats[n % 2, panels * at : panels * (at + 1), :] = (
+                mats[n % 4, panels * at : panels * (at + 1), :] = (
                     lax.rsqrt(squared) * w
                 ).astype(BF16)
 
@@ -450,12 +450,13 @@
             s, h, i = work[n]
             l, ks = leaves(h, i)
             wide = jnp.concatenate([hsrc[s, k] for k, _ in ks], axis=1)
-            acc[t, l] += dot(wide, mats[n % 2, 0 : panels * len(ks), :])
+            acc[t, l] += dot(wide, mats[n % 4, 0 : panels * len(ks), :])
 
         fill(0)
+        fill(1)
         for n in range(len(work)):
-            if n + 1 < len(work):
-                fill(n + 1)
+            if n + 2 < len(work):
+                fill(n + 2)
             apply(n)
 
     own_couplings()
@@ -575,7 +576,7 @@
             pltpu.VMEM((n_gy, 8, max(128, 8 * n_gx)), F32),
             pltpu.VMEM((8, max(128, 8 * n_gx)), F32),
             pltpu.VMEM((4, 8, max(128, 8 * n_gx)), F32),
-            pltpu.VMEM((2, 3 * panels, panels), BF16),
+            pltpu.VMEM((4, 3 * panels, panels), BF16),
             pltpu.VMEM((64, 2 * rhs), F32),
             pltpu.VMEM((n_gy, 64, 2 * rhs), F32),
             pltpu.VMEM((48, 2 * rhs), F32),

time: 26.3 us -> 25.9 us (0.985)
  Pallas kernels: 24 us -> 23.5 us
    pallas_call x1, Pallas kernels: 24 us -> 23.5 us  [body(): pl.pallas_call(functools.partial(kernel, n_gx, n_gy), out_shape=(jax.Shap...]
where the time goes in v7:
time: 25.9 us; the launch traced here: 25.6 us
  Pallas kernels  23.5 us (91%)
  other arithmetic  2.06 us (8%)
    pallas_call x1, Pallas kernels, body(): pl.pallas_call(functools.partial(kernel, n_gx, n_gy), out_shape=(jax.Shap...  23.5 us
    reshape x1, other arithmetic, body(): return potential.reshape(sources.shape)  2.06 us

profile of v7, /device:TPU:1, one launch (start us, length us, event | category | flops | bytes accessed | tf_op | source)
XLA Modules:
  0.0 25.6 jit_solution(18155170689890714694)
XLA Ops:
  0.0 23.5 %shard_map.73 = (f32[8,64,256]{2,1,0:T(8,128)}, bf16[2,8,64,256]{3,2,1,0:T(8,128)(2,1)}) custom-call(bf16[8,64,256]{2,1,0:T(8,128)(2,1)} %bitcast.15, bf16[8,4,256]{2,1,0:T(4,128)(2,1)} %bitcast.17, s32[8,24]{1,0:T(8,128)} %bitcast.18, s32[4,16]{1,0:T(4,128)} %bitcast.19, bf16[1024,256]{1,0:T(8,128)(2,1)} %bitcast.13, bf16[1024,256]{1,0:T(8,128)(2,1)} %bitcast.14, ...), custom_call_target="tpu_custom_call" | custom-call | tf_op jit(solution)/shard_map/pallas_call | solution.py:545
  23.5 2.1 %fusion = f32[1,1,8,64,256]{4,3,2,1,0:T(8,128)} fusion(f32[8,64,256]{2,1,0:T(8,128)} %get-tuple-element.7, bf16[2,8,64,256]{3,2,1,0:T(8,128)(2,1)} %get-tuple-element.8), kind=kLoop, calls=%fused_computation.1 | loop fusion | flops 524288 | bytes 1572864 | tf_op jit(solution)/shard_map/reshape | solution.py:605
